TPU v7x, 32 devices: a whole 2x2x4 slice. The times are simulated.
32 devices in a mesh: groups: 2 (over y), tp: 4 (over x, core), pool: 4 (over z).
Axes of the slice: x: 2, y: 2, z: 4, core: 2. Of those that a mesh axis runs over, the one named last changes fastest.
Arguments:
- frames: bfloat16 [4096, 5120], P(('groups', 'pool'), 'tp'), parts along dimension 0, may hold values from -6 to 6
- norm_gain: bfloat16 [5120], P('tp'), may hold values from 0.099609375 to 1.8984375
- kv_weight: bfloat16 [5120, 2048], P('tp'), may hold values from -0.078125 to 0.078125
- kv_cache: bfloat16 [32768, 2048], P(('groups', 'tp', 'pool')), parts along dimension 0, may hold values from -6 to 6
- queries: bfloat16 [64, 4096], P(('groups', 'tp', 'pool')), parts along dimension 0, may hold values from -12 to 12
- placement: int32 [64], P('groups'), parts along dimension 0, may hold values from 0 to 31, as said below
- cached_len: int32 [64], P('groups'), parts along dimension 0, may hold values from 64 to 512
- frame_count: int32 [64], P('groups'), parts along dimension 0, may hold values from 1 to 64
Outputs:
- attended: bfloat16 [64, 4096], P(('groups', 'tp', 'pool')), parts along dimension 0
There are 2 independent parts, one for each index of `groups`. A program takes and returns all parts, laid end to end along the dimension named above; an argument that names none is the same for every part. Nothing has to cross between parts.
Inputs may be any that keep to these rules, and one draw needn't show every extreme that they name: placement[s] = owner * 2 + slot, where owner counts devices along tp and pool with tp slowest; no two sessions share a row; the 8 consecutive sessions of one prefill group have different owners, and exactly 2 of them have owners with any given pool index; every owner holds no session or 2 of them.
All inputs are finite; a program needn't handle non-finite values.
Results may differ from a plain program's by a relative error of at most 0.007.
Values may be sent and summed in bfloat16 or wider, within the bound.
A program may use at most 128 MiB of HBM per device.

v0:
```python
import jax
import jax.numpy as jnp
from jax import lax
from jax.sharding import PartitionSpec as P

D = 5120
QH = 32
KVH = 8
HD = 128
FRAMES = 64
SLOT_TOK = 512


def split_heads(stacked, slot_count):
    head_span = KVH * HD
    keys_part = stacked[:, :, :head_span].reshape(slot_count, -1, KVH, HD)
    values_part = stacked[:, :, head_span:].reshape(slot_count, -1, KVH, HD)
    return (keys_part, values_part)


def per_device(frames, norm_gain, kv_weight, kv_cache, queries, placement, cached_len, frame_count):
    tensor_count = lax.axis_size("tp")
    pool_count = lax.axis_size("pool")
    row_count = frames.shape[0]
    width_local = frames.shape[1]
    kv_width = kv_weight.shape[1]
    block_width = kv_width // tensor_count
    sessions_here = row_count // FRAMES
    tensor_index = lax.axis_index("tp")
    pool_index = lax.axis_index("pool")
    slot_count = queries.shape[0]
    owner_count = tensor_count * pool_count
    session_total = placement.shape[0]
    session_ids = jnp.arange(session_total, dtype=jnp.int32)
    owner_all = placement // slot_count
    group_all = session_ids // sessions_here
    first_local = pool_index * sessions_here
    my_owner = tensor_index * pool_count + pool_index
    wanted = my_owner * slot_count + jnp.arange(slot_count, dtype=jnp.int32)
    holder = placement[None, :] == wanted[:, None]
    columns = lax.all_to_all(kv_weight, "tp", split_axis=1, concat_axis=0, tiled=True)
    portion = lax.all_gather(frames, "tp", axis=1, tiled=True)
    gain_portion = lax.all_gather(norm_gain.reshape(1, width_local), "tp", axis=1, tiled=True)
    widened = portion.astype(jnp.float32)
    scaled = (widened * gain_portion.astype(jnp.float32)).astype(jnp.bfloat16)
    product = jnp.dot(scaled, columns, preferred_element_type=jnp.float32)
    product, squares = (product, jnp.sum(widened * widened, axis=1))
    inverse = lax.rsqrt(squares / D + 1e-06)
    fresh_rows = (product * inverse[:, None]).astype(jnp.bfloat16)
    fresh_flat = fresh_rows.reshape(sessions_here, FRAMES * block_width)
    local_owner = lax.dynamic_slice_in_dim(owner_all, first_local, sessions_here)
    targets = jnp.arange(owner_count, dtype=jnp.int32)
    picker = (local_owner[None, :] == targets[:, None]).astype(jnp.bfloat16)
    outgoing = jnp.dot(picker, fresh_flat, preferred_element_type=jnp.float32).astype(jnp.bfloat16)
    incoming = lax.all_to_all(outgoing, ("tp", "pool"), split_axis=0, concat_axis=0, tiled=True)
    source_group = jnp.sum(jnp.where(holder, group_all[None, :], 0), axis=1)
    selector = (source_group[:, None] == jnp.arange(pool_count, dtype=jnp.int32)[None, :]).astype(
        jnp.bfloat16
    )
    arranged = jnp.einsum(
        "jq,tqx->jtx",
        selector,
        incoming.reshape(tensor_count, pool_count, FRAMES * block_width),
        preferred_element_type=jnp.float32,
    ).astype(jnp.bfloat16)
    arrived = arranged.reshape(slot_count, tensor_count, FRAMES, block_width).transpose(0, 2, 1, 3)
    fresh_slots = arrived.reshape(slot_count, FRAMES, kv_width)
    occupied = jnp.any(holder, axis=1)
    cached_count = jnp.sum(jnp.where(holder, cached_len[None, :], 0), axis=1)
    fresh_count = jnp.sum(jnp.where(holder, frame_count[None, :], 0), axis=1)
    group_size = QH // KVH
    query_heads = queries.reshape(slot_count, KVH, group_size, HD)
    cache_slots = kv_cache.reshape(slot_count, SLOT_TOK, kv_width)
    old_keys, old_values = split_heads(cache_slots, slot_count)
    new_keys, new_values = split_heads(fresh_slots, slot_count)
    score_scale = HD ** (-0.5)
    old_scores = (
        jnp.einsum("skgd,stkd->skgt", query_heads, old_keys, preferred_element_type=jnp.float32)
        * score_scale
    )
    new_scores = (
        jnp.einsum("skgd,stkd->skgt", query_heads, new_keys, preferred_element_type=jnp.float32)
        * score_scale
    )
    old_valid = (
        jnp.arange(SLOT_TOK, dtype=jnp.int32)[None, None, None, :]
        < cached_count[:, None, None, None]
    )
    new_valid = (
        jnp.arange(FRAMES, dtype=jnp.int32)[None, None, None, :] < fresh_count[:, None, None, None]
    )
    old_scores = jnp.where(old_valid, old_scores, -1e30)
    new_scores = jnp.where(new_valid, new_scores, -1e30)
    highest = jnp.maximum(
        jnp.max(old_scores, axis=-1, keepdims=True), jnp.max(new_scores, axis=-1, keepdims=True)
    )
    old_exp = jnp.exp(old_scores - highest)
    new_exp = jnp.exp(new_scores - highest)
    denominator = jnp.sum(old_exp, axis=-1, keepdims=True) + jnp.sum(
        new_exp, axis=-1, keepdims=True
    )
    old_weights = (old_exp / denominator).astype(jnp.bfloat16)
    new_weights = (new_exp / denominator).astype(jnp.bfloat16)
    attended = jnp.einsum(
        "skgt,stkd->skgd", old_weights, old_values, preferred_element_type=jnp.float32
    )
    attended = attended + jnp.einsum(
        "skgt,stkd->skgd", new_weights, new_values, preferred_element_type=jnp.float32
    )
    attended = attended * occupied.astype(jnp.float32)[:, None, None, None]
    return attended.reshape(slot_count, QH * HD).astype(jnp.bfloat16)


def solution(mesh):
    return jax.shard_map(
        per_device,
        mesh=mesh,
        in_specs=(
            P(("groups", "pool"), "tp"),
            P("tp"),
            P("tp", None),
            P(("groups", "tp", "pool"), None),
            P(("groups", "tp", "pool"), None),
            P("groups"),
            P("groups"),
            P("groups"),
        ),
        out_specs=P(("groups", "tp", "pool"), None),
        check_vma=False,
    )
```

profile of v0, /device:TPU:0, one launch (start us, length us, event | category | flops | bytes accessed | tf_op | source)
XLA Modules:
  0.0 182.1 jit_solution(10883355285063771149)
XLA Ops:
  6.5 0.7 all-gather.4.cloned.1.call-update
  7.3 7.9 %copy.45 = bf16[1280,2048]{0,1:T(8,128)(2,1)} copy(bf16[1280,2048]{1,0:T(8,128)(2,1)} %param.10) | data formatting | bytes 10485760 | tf_op args[2]
  15.1 5.3 %all-to-all-start = ((bf16[1280,4,512]{0,2,1:T(8,128)(2,1)}), bf16[1280,4,512]{0,2,1:T(8,128)(2,1)}, u32[]{:S(2)}, u32[]{:S(2)}) async-start(bf16[1280,4,512]{0,2,1:T(8,128)(2,1)} %bitcast.38), calls=%async_computation | async-start | bytes 10485760 | tf_op jit(solution)/shard_map/all_to_all | solution.py:41
  20.5 87.2 %all-gather.1 = bf16[4,1,1280]{2,1,0:T(2,128)(2,1)S(1)} all-gather(bf16[1,1,1280]{2,1,0:T(2,128)(2,1)S(1)} %reshape.140), channel_id=2, replica_groups=mesh['groups'=2,'tp'=4,'pool'=4] {'tp'}, dimensions={0}, use_global_device_ids=true | all-gather | bytes 12800 | tf_op jit(solution)/shard_map/all_gather | solution.py:43
  107.8 7.9 %copy.46 = bf16[4,1280,512]{2,1,0:T(8,128)(2,1)} copy(bf16[4,1280,512]{1,2,0:T(8,128)(2,1)} %bitcast.5) | data formatting | bytes 10485760 | tf_op jit(solution)/shard_map/all_to_all | solution.py:41
  115.7 3.7 %fusion.2 = f32[512]{0:T(512)S(1)} fusion(bf16[512,5120]{1,0:T(8,128)(2,1)} %all-gather.4.cloned.1.call-done), kind=kLoop, calls=%fused_computation.6 | loop fusion | flops 7863808 | bytes 5244928 | tf_op jit(solution)/shard_map/reduce_sum | solution.py:47
  119.7 5.4 %fusion.9 = bf16[512,512]{1,0:T(8,128)(2,1)S(1)} fusion(bf16[5120,512]{1,0:T(8,128)(2,1)} %bitcast.41, bf16[512,5120]{1,0:T(8,128)(2,1)S(1)} %copy-done.1, f32[5120]{0:T(1024)S(1)} %bitcast.44, f32[512]{0:T(512)S(1)} %add_rsqrt_fusion), kind=kOutput, calls=%fused_computation.10 | convolution fusion | flops 2692743168 | bytes 11032576 | tf_op jit(solution)/shard_map/dot_general | solution.py:46
  125.3 0.4 fusion
  125.8 0.5 broadcast.85
  126.3 1.4 reduce.1
  127.7 1.6 reshape.145
  129.3 4.7 %all-to-all-start.1 = ((bf16[16,2,16384]{2,1,0:T(2,128)(2,1)}), bf16[16,2,16384]{2,1,0:T(2,128)(2,1)S(1)}, u32[]{:S(2)}, u32[]{:S(2)}) async-start(bf16[16,2,16384]{2,1,0:T(2,128)(2,1)} %reshape.145), calls=%async_computation.1 | async-start | bytes 2097152 | tf_op jit(solution)/shard_map/all_to_all | solution.py:55
  134.1 4.2 %fusion.36 = (bf16[2,512,1024]{2,1,0:T(8,128)(2,1)}, bf16[2,512,1024]{2,1,0:T(8,128)(2,1)S(1)}) fusion(bf16[2,512,2048]{2,1,0:T(8,128)(2,1)} %bitcast.42), kind=kLoop, calls=%fused_computation.62 | loop fusion | bytes 8388608 | tf_op jit(solution)/shard_map/slice | solution.py:16
  138.3 2.6 %copy.50 = bf16[2,512,1024]{1,2,0:T(8,128)(2,1)} copy(bf16[2,512,1024]{2,1,0:T(8,128)(2,1)S(1)} %get-tuple-element.9) | data formatting | bytes 4194304 | tf_op jit(solution)/shard_map/slice | solution.py:17
  140.8 2.9 %copy.43 = bf16[2,512,1024]{1,2,0:T(8,128)(2,1)S(1)} copy(bf16[2,512,1024]{2,1,0:T(8,128)(2,1)} %get-tuple-element.8) | data formatting | bytes 4194304 | tf_op jit(solution)/shard_map/slice | solution.py:16
  144.3 0.5 fusion.37
  144.8 16.2 %all-to-all-done.1 = bf16[16,2,16384]{2,1,0:T(2,128)(2,1)S(1)} async-done(((bf16[16,2,16384]{2,1,0:T(2,128)(2,1)}), bf16[16,2,16384]{2,1,0:T(2,128)(2,1)S(1)}, u32[]{:S(2)}, u32[]{:S(2)}) %all-to-all-start.1) | async-done | bytes 1048608 | tf_op jit(solution)/shard_map/all_to_all | solution.py:55
  161.0 1.0 reshape.146
  162.1 6.4 %reduce = bf16[16,32768]{1,0:T(8,128)(2,1)S(1)} reduce(bf16[16,1,32768]{2,1,0:T(2,128)(2,1)S(1)} %reshape.146, bf16[]{:T(256)} %constant.58), dimensions={1}, to_apply=%all_to_all.25.reduce_sub_computation | reduce | bytes 2097154 | tf_op jit(solution)/shard_map/all_to_all | solution.py:55
  168.5 1.2 reshape.130
  169.7 2.0 %convolution_convert_fusion.1 = bf16[2,4,32768]{2,0,1:T(2,128)(2,1)S(1)} fusion(bf16[4,4,32768]{2,1,0:T(4,128)(2,1)} %reshape.130, s32[2]{0:T(128)S(1)} %get-tuple-element.6), kind=kOutput, calls=%fused_computation.2 | convolution fusion | flops 2359304 | bytes 1572872 | tf_op jit(solution)/shard_map/jq,tqx->jtx/dot_general | solution.py:60
  172.1 0.4 copy.69
  173.6 0.7 fusion.22
  174.6 0.6 convert_element_type.46
  (40 shorter events, 3.0 us)
Async XLA Ops:
  6.5 109.1 %all-gather.4.cloned.1.call-start = ((), (), s32[]{:S(2)}) async-start(), calls=%async_computation.2 | async-start | bytes 6553600 | tf_op jit(solution)/shard_map/all_gather | solution.py:42
  15.1 5.4 %copy-start.3 = (bf16[1280]{0:T(1024)(128)(2,1)S(1)}, bf16[1280]{0:T(1024)(128)(2,1)}, u32[]{:S(2)}) copy-start(bf16[1280]{0:T(1024)(128)(2,1)} %param.9) | copy-start | bytes 7684
  15.1 92.6 %copy-start.5 = (s32[32]{0:T(128)S(1)}, s32[32]{0:T(128)}, u32[]{:S(2)}) copy-start(s32[32]{0:T(128)} %param.13) | copy-start | bytes 388
  15.1 92.7 %all-to-all-start = ((bf16[1280,4,512]{0,2,1:T(8,128)(2,1)}), bf16[1280,4,512]{0,2,1:T(8,128)(2,1)}, u32[]{:S(2)}, u32[]{:S(2)}) async-start(bf16[1280,4,512]{0,2,1:T(8,128)(2,1)} %bitcast.38), calls=%async_computation | async-start | bytes 10485760 | tf_op jit(solution)/shard_map/all_to_all | solution.py:41
  115.7 4.0 %copy-start.1 = (bf16[512,5120]{1,0:T(8,128)(2,1)S(1)}, bf16[512,5120]{1,0:T(8,128)(2,1)}, u32[]{:S(2)}) copy-start(bf16[512,5120]{1,0:T(8,128)(2,1)} %all-gather.4.cloned.1.call-done) | copy-start | bytes 15728644
  129.3 31.7 %all-to-all-start.1 = ((bf16[16,2,16384]{2,1,0:T(2,128)(2,1)}), bf16[16,2,16384]{2,1,0:T(2,128)(2,1)S(1)}, u32[]{:S(2)}, u32[]{:S(2)}) async-start(bf16[16,2,16384]{2,1,0:T(2,128)(2,1)} %reshape.145), calls=%async_computation.1 | async-start | bytes 2097152 | tf_op jit(solution)/shard_map/all_to_all | solution.py:55
  134.1 6.8 %copy-start.2 = (bf16[2,4096]{1,0:T(2,128)(2,1)S(1)}, bf16[2,4096]{1,0:T(2,128)(2,1)}, u32[]{:S(2)}) copy-start(bf16[2,4096]{1,0:T(2,128)(2,1)} %param.12) | copy-start | bytes 49156
  138.3 5.7 %copy-start.4 = (s32[32]{0:T(128)S(1)}, s32[32]{0:T(128)}, u32[]{:S(2)}) copy-start(s32[32]{0:T(128)} %param.15) | copy-start | bytes 388
  138.3 5.7 %copy-start.6 = (s32[32]{0:T(128)S(1)}, s32[32]{0:T(128)}, u32[]{:S(2)}) copy-start(s32[32]{0:T(128)} %param.14) | copy-start | bytes 388
  168.5 5.2 %copy-start = (bf16[2,512,1024]{1,2,0:T(8,128)(2,1)S(1)}, bf16[2,512,1024]{1,2,0:T(8,128)(2,1)}, u32[]{:S(2)}) copy-start(bf16[2,512,1024]{1,2,0:T(8,128)(2,1)} %copy.50) | copy-start | bytes 6291460
Sparse Core Ops, SparseCore 0:
  8.9 69.2 all-gather.3
where the time goes:
time: 183 us; the launch traced here: 182 us
  blocking collectives  87.2 us (48%)
  local copies, waits for them, and re-layouts  32.2 us (18%)
  waiting for transfers between devices  17 us (9%)
  between operations  13.6 us (7%)
  other arithmetic  12.5 us (7%)
  starting transfers between devices  10.1 us (6%)
  matrix products  9.52 us (5%)
    all_gather x1, blocking collectives, per_device(): lax.all_gather(norm_gain.reshape(1, width_local), 'tp', axis=1, tiled=True)  87.2 us
    all_to_all x1, waiting for transfers between devices, per_device(): lax.all_to_all(outgoing, ('tp', 'pool'), split_axis=0, concat_axis=0, til...  16.2 us
    unnamed x19, local copies, waits for them, and re-layouts  10.9 us
    all_to_all x1, local copies, waits for them, and re-layouts, per_device(): lax.all_to_all(kv_weight, 'tp', split_axis=1, concat_axis=0, tiled=True)  7.87 us
    all_to_all x2, other arithmetic, per_device(): lax.all_to_all(outgoing, ('tp', 'pool'), split_axis=0, concat_axis=0, til...  7.82 us
    slice x2, local copies, waits for them, and re-layouts, split_heads(): keys_part = stacked[:, :, :head_span].reshape(slot_count, -1, KVH, HD)  7.03 us
    dot_general x1, matrix products, per_device(): product = jnp.dot(scaled, columns, preferred_element_type=jnp.float32)  5.39 us
    all_to_all x1, starting transfers between devices, per_device(): lax.all_to_all(kv_weight, 'tp', split_axis=1, concat_axis=0, tiled=True)  5.33 us
  transfers between devices with their start and end apart: 3, of which 1 were waited for; matrix products, arithmetic and copies ran while one was open for 15% of the time, Pallas kernels for 0%

commit v1 on v0

v1 whole, which is shorter than its diff:
```python
import functools

import jax
import jax.numpy as jnp
from jax import lax
from jax.experimental import pallas as pl
from jax.experimental.pallas import tpu as pltpu
from jax.sharding import PartitionSpec as P

QH = 32
KVH = 8
HD = 128
GRP = QH // KVH
HS = KVH * HD
FRAMES = 64
SLOT_TOK = 512
PACK = 128 // QH
F32 = jnp.float32
BF = jnp.bfloat16
NT = (((1,), (1,)), ((), ()))
TN = (((0,), (0,)), ((), ()))


def iota(shape, dim):
    return lax.broadcasted_iota(jnp.int32, shape, dim)


def spread_heads(rows):
    wide = jnp.concatenate([rows.astype(F32)] * KVH, axis=1)
    own = (iota(wide.shape, 0) % QH) // GRP == iota(wide.shape, 1) // HD
    return jnp.where(own, wide, 0.0).astype(BF)


def gather_heads(wide):
    head = (iota((wide.shape[0], HD), 0) % QH) // GRP
    out = jnp.zeros((wide.shape[0], HD), F32)
    for j in range(KVH):
        out = jnp.where(head == j, wide[:, j * HD:(j + 1) * HD], out)
    return out


def permute(picks, blocks):
    shape = (QH, blocks.shape[0])
    offset = iota(shape, 1) - iota(shape, 0)
    hot = jnp.concatenate([jnp.where(offset == pick * QH, 1.0, 0.0) for pick in picks], axis=0)
    return jnp.dot(hot.astype(BF), blocks, preferred_element_type=F32).astype(BF)


def kernel(n_tp, n_pool, place, clen, fcnt, gain, q, frames_h, w_h, cache_h, out,
           fr, wk, wv, ca, xs, qt, qg, sendq, recvq, ssq, sg, lse, ob, sendo, recvo,
           sendp, recvp, oc,
           ld, s_tp, r_tp, s_pl, r_pl):
    slots = q.shape[0] // QH
    n_loc = fr.shape[0] // FRAMES
    per = n_loc // n_pool
    tiles = n_loc // PACK
    width = fr.shape[1]
    scale = HD ** -0.5
    t = lax.axis_index("tp")
    p = lax.axis_index("pool")

    loads = [
        pltpu.make_async_copy(frames_h, fr, ld.at[0]),
        pltpu.make_async_copy(w_h.at[:, pl.ds(0, HS)], wk, ld.at[1]),
        pltpu.make_async_copy(cache_h, ca, ld.at[2]),
        pltpu.make_async_copy(w_h.at[:, pl.ds(HS, HS)], wv, ld.at[3]),
    ]
    for c in loads:
        c.start()

    barrier = pltpu.get_barrier_semaphore()
    for d in range(1, n_tp):
        pl.semaphore_signal(barrier, inc=1, device_id={"tp": lax.rem(t + d, n_tp)},
                            device_id_type=pl.DeviceIdType.MESH)
    for d in range(1, n_pool):
        pl.semaphore_signal(barrier, inc=1, device_id={"pool": lax.rem(p + d, n_pool)},
                            device_id_type=pl.DeviceIdType.MESH)

    def to_tp(stage, src, dst):
        made = []
        for d in range(1, n_tp):
            peer = lax.rem(t + d, n_tp)
            made.append(pltpu.make_async_remote_copy(
                src_ref=src(peer), dst_ref=dst, send_sem=s_tp.at[stage, d],
                recv_sem=r_tp.at[stage, d], device_id={"tp": peer},
                device_id_type=pl.DeviceIdType.MESH))
        for c in made:
            c.start()
        return made

    def to_pool(stage, src, dst):
        made = []
        for d in range(1, n_pool):
            peer = lax.rem(p + d, n_pool)
            made.append(pltpu.make_async_remote_copy(
                src_ref=src(peer), dst_ref=dst, send_sem=s_pl.at[stage, d],
                recv_sem=r_pl.at[stage, d], device_id={"pool": peer},
                device_id_type=pl.DeviceIdType.MESH))
        for c in made:
            c.start()
        return made

    qg[t] = q[...]
    pl.semaphore_wait(barrier, n_tp - 1 + n_pool - 1)
    hop = to_tp(0, lambda peer: qg.at[t], qg.at[t])

    keys = []
    for g in range(n_pool):
        found = [jnp.int32(0)] * per
        count = jnp.int32(0)
        for s in range(g * n_loc, (g + 1) * n_loc):
            row = place[s]
            owner = row // slots
            match = owner % n_pool == p
            key = (owner // n_pool) * slots + row % slots
            for k in range(per):
                found[k] = jnp.where(match & (count == k), key, found[k])
            count = count + match.astype(jnp.int32)
        keys += found
    held = []
    for o in range(n_tp * slots):
        which = jnp.int32(-1)
        for c in range(n_pool * per):
            which = jnp.where(keys[c] == o, c, which)
        held.append(which)
    counts = [jnp.int32(0)] * n_pool
    order = [jnp.int32(0)] * n_loc
    for s in range(n_loc):
        column = (place[p * n_loc + s] // slots) % n_pool
        for c in range(n_pool):
            match = column == c
            for k in range(per):
                u = c * per + k
                order[u] = jnp.where(match & (counts[c] == k), s, order[u])
            counts[c] = counts[c] + match.astype(jnp.int32)
    lengths, mine = [], []
    for i in range(slots):
        length = jnp.int32(0)
        for s in range(n_pool * n_loc):
            length = jnp.where(place[s] == (t * n_pool + p) * slots + i, clen[s], length)
        which = jnp.int32(-1)
        for c in range(n_pool * per):
            which = jnp.where(keys[c] == t * slots + i, c, which)
        lengths.append(length)
        mine.append(which)

    loads[0].wait()
    gain_row = gain[...].astype(F32)
    lane = iota((FRAMES, 128), 1)

    def scale_session(s, total):
        x = fr[s * FRAMES:(s + 1) * FRAMES, :].astype(F32)
        xs[s * FRAMES:(s + 1) * FRAMES, :] = (x * gain_row).astype(BF)
        return jnp.where(lane == s, jnp.sum(x * x, axis=1, keepdims=True), total)

    total = jnp.zeros((FRAMES, 128), F32)
    for s in range(n_loc // 2):
        total = scale_session(s, total)

    for c in hop:
        c.wait()
    moved = permute(keys, qg[...].reshape(n_tp * slots * QH, HD))
    sendq[...] = moved.reshape(n_pool, per * QH, HD)
    recvq[p] = sendq[p]
    hop = to_pool(0, lambda peer: sendq.at[peer], recvq.at[p])

    for s in range(n_loc // 2, n_loc):
        total = scale_session(s, total)
    ssq[t] = total
    hop_sq = to_tp(1, lambda peer: ssq.at[t], ssq.at[t])
    loads[1].wait()
    for c in hop:
        c.wait()

    who = []
    group = recvq[...].reshape(n_loc * QH, HD)
    for a in range(tiles):
        ids = jnp.zeros((FRAMES, 128), jnp.int32)
        for k in range(PACK):
            ids = jnp.where(lane // QH == k, order[a * PACK + k], ids)
        who.append(ids)
        qt[:, a * 128:(a + 1) * 128] = lax.dot_general(
            wk[...], spread_heads(group[a * 128:(a + 1) * 128]), NT,
            preferred_element_type=F32).astype(BF)
    full = jnp.dot(xs[...], qt[...], preferred_element_type=F32)
    for a in range(tiles):
        packed = jnp.zeros((FRAMES, 128), F32)
        for s in range(n_loc):
            packed = jnp.where(who[a] == s, full[s * FRAMES:(s + 1) * FRAMES, a * 128:(a + 1) * 128],
                               packed)
        sg[t, a * FRAMES:(a + 1) * FRAMES, :] = packed
    hop = to_tp(2, lambda peer: sg.at[t], sg.at[t])

    loads[2].wait()
    tops, sums = [], []
    for i in range(slots):
        qb = spread_heads(q[i * QH:(i + 1) * QH, :])
        rows = slice(i * SLOT_TOK, (i + 1) * SLOT_TOK)
        sc = lax.dot_general(qb, ca[rows, :HS], NT, preferred_element_type=F32) * scale
        sc = jnp.where(iota(sc.shape, 1) < lengths[i], sc, -1e30)
        top = jnp.max(sc, axis=1, keepdims=True)
        pr = jnp.exp(sc - top)
        tops.append(top)
        sums.append(jnp.sum(pr, axis=1, keepdims=True))
        oc[i * QH:(i + 1) * QH, :] = gather_heads(
            jnp.dot(pr.astype(BF), ca[rows, HS:], preferred_element_type=F32))

    for c in hop_sq:
        c.wait()
    squares = ssq[0]
    for j in range(1, n_tp):
        squares = squares + ssq[j]
    inverse = lax.rsqrt(squares / (width * n_tp) + 1e-06)
    for c in hop:
        c.wait()
    weights = []
    for a in range(tiles):
        inv = jnp.zeros((FRAMES, 128), F32)
        valid = jnp.zeros((FRAMES, 128), jnp.int32)
        for s in range(n_loc):
            inv = jnp.where(who[a] == s, inverse[:, s:s + 1], inv)
            valid = jnp.where(who[a] == s, fcnt[p * n_loc + s], valid)
        sc = sg[0, a * FRAMES:(a + 1) * FRAMES, :]
        for j in range(1, n_tp):
            sc = sc + sg[j, a * FRAMES:(a + 1) * FRAMES, :]
        sc = jnp.where(iota(sc.shape, 0) < valid, sc * (inv * scale), -1e30)
        top = jnp.max(sc, axis=0, keepdims=True)
        pr = jnp.exp(sc - top)
        norm = jnp.sum(pr, axis=0, keepdims=True)
        lse[p, a:a + 1, :] = top + jnp.log(norm)
        weights.append(pr * inv / norm)
    if tiles < lse.shape[1]:
        lse[p, tiles:, :] = jnp.zeros((lse.shape[1] - tiles, 128), F32)
    hop_l = to_pool(1, lambda peer: lse.at[p], lse.at[p])

    loads[3].wait()
    for a in range(tiles):
        wide = jnp.concatenate(
            [jnp.where(who[a] == s, weights[a], 0.0) for s in range(n_loc)], axis=0)
        y = jnp.dot(wide.T.astype(BF), xs[...], preferred_element_type=F32).astype(BF)
        ob[a * 128:(a + 1) * 128, :] = gather_heads(
            jnp.dot(y, wv[...], preferred_element_type=F32)).astype(BF)
    sendo[...] = ob[...].reshape(n_pool, per * QH, HD)
    recvo[p] = sendo[p]
    hop = to_pool(2, lambda peer: sendo.at[peer], recvo.at[p])
    for c in hop_l:
        c.wait()
    fresh_lse = []
    offset = iota((QH, 128), 1) - iota((QH, 128), 0)
    for i in range(slots):
        spread = jnp.zeros((QH, 128), F32)
        for c in range(n_pool * per):
            u = p * per + c % per
            line = lse[c // per, pl.ds(u // PACK, 1), :]
            here = (offset == (u % PACK) * QH) & (mine[i] == c)
            spread = jnp.where(here, line, spread)
        fresh_lse.append(jnp.sum(spread, axis=1, keepdims=True))
    for c in hop:
        c.wait()

    moved = permute(held, recvo[...].reshape(n_loc * QH, HD))
    sendp[...] = moved.reshape(n_tp, slots * QH, HD)
    recvp[t] = sendp[t]
    hop = to_tp(3, lambda peer: sendp.at[peer], recvp.at[t])
    for c in hop:
        c.wait()
    for i in range(slots):
        rows = slice(i * QH, (i + 1) * QH)
        new = recvp[0, rows, :].astype(F32)
        for j in range(1, n_tp):
            new = new + recvp[j, rows, :].astype(F32)
        top = jnp.maximum(tops[i], fresh_lse[i])
        ea = jnp.exp(fresh_lse[i] - top)
        eb = jnp.exp(tops[i] - top)
        res = (ea * new + eb * oc[rows, :]) / (ea + eb * sums[i])
        out[rows, :] = jnp.where(mine[i] >= 0, res, 0.0).astype(BF)


def per_device(n_tp, n_pool, frames, norm_gain, kv_weight, kv_cache, queries, placement,
               cached_len, frame_count):
    rows, width = frames.shape
    slots = queries.shape[0]
    n_loc = rows // FRAMES
    per = n_loc // n_pool
    tiles = n_loc // PACK
    vm = pl.BlockSpec(memory_space=pltpu.VMEM)
    sm = pl.BlockSpec(memory_space=pltpu.SMEM)
    hbm = pl.BlockSpec(memory_space=pltpu.HBM)
    out = pl.pallas_call(
        functools.partial(kernel, n_tp, n_pool),
        out_shape=jax.ShapeDtypeStruct((slots * QH, HD), BF),
        in_specs=[sm, sm, sm, vm, vm, hbm, hbm, hbm],
        out_specs=vm,
        scratch_shapes=[
            pltpu.VMEM((rows, width), BF),
            pltpu.VMEM((width, HS), BF),
            pltpu.VMEM((width, HS), BF),
            pltpu.VMEM(kv_cache.shape, BF),
            pltpu.VMEM((rows, width), BF),
            pltpu.VMEM((width, n_loc * QH), BF),
            pltpu.VMEM((n_tp, slots * QH, HD), BF),
            pltpu.VMEM((n_pool, per * QH, HD), BF),
            pltpu.VMEM((n_pool, per * QH, HD), BF),
            pltpu.VMEM((n_tp, FRAMES, 128), F32),
            pltpu.VMEM((n_tp, tiles * FRAMES, 128), F32),
            pltpu.VMEM((n_pool, max(8, tiles), 128), F32),
            pltpu.VMEM((n_loc * QH, HD), BF),
            pltpu.VMEM((n_pool, per * QH, HD), BF),
            pltpu.VMEM((n_pool, per * QH, HD), BF),
            pltpu.VMEM((n_tp, slots * QH, HD), BF),
            pltpu.VMEM((n_tp, slots * QH, HD), BF),
            pltpu.VMEM((slots * QH, HD), F32),
            pltpu.SemaphoreType.DMA((4,)),
            pltpu.SemaphoreType.DMA((4, n_tp)),
            pltpu.SemaphoreType.DMA((4, n_tp)),
            pltpu.SemaphoreType.DMA((3, n_pool)),
            pltpu.SemaphoreType.DMA((3, n_pool)),
        ],
        compiler_params=pltpu.CompilerParams(
            collective_id=0, has_side_effects=True, vmem_limit_bytes=62 * 1024 * 1024),
    )(placement, cached_len, frame_count, norm_gain.reshape(1, width),
      queries.reshape(slots * QH, HD), frames, kv_weight, kv_cache)
    return out.reshape(slots, QH * HD)


def solution(mesh):
    return jax.shard_map(
        functools.partial(per_device, mesh.shape["tp"], mesh.shape["pool"]),
        mesh=mesh,
        in_specs=(
            P(("groups", "pool"), "tp"),
            P("tp"),
            P("tp", None),
            P(("groups", "tp", "pool"), None),
            P(("groups", "tp", "pool"), None),
            P("groups"),
            P("groups"),
            P("groups"),
        ),
        out_specs=P(("groups", "tp", "pool"), None),
        check_vma=False,
    )
```

time: 183 us -> 32.5 us (0.18)
  blocking collectives: 87.2 us -> 0 us
  local copies, waits for them, and re-layouts: 32.2 us -> 3.95 us
  Pallas kernels: 0 us -> 28.1 us
  waiting for transfers between devices: 17 us -> 0 us
  between operations: 13.6 us -> 0.01 us
  other arithmetic: 12.5 us -> 0 us
  starting transfers between devices: 10.1 us -> 0 us
  matrix products: 9.52 us -> 0 us
    all_gather x1 -> x0, blocking collectives: 87.2 us -> none  [per_device(): lax.all_gather(norm_gain.reshape(1, width_local), 'tp', axis=1, tiled=True)]
    pallas_call x0 -> x1, Pallas kernels: none -> 28.1 us  [per_device(): pl.pallas_call(functools.partial(kernel, n_tp, n_pool), out_shape=jax.Sha...]
    all_to_all x2 -> x0, waiting for transfers between devices: 16.3 us -> none  [the longest x1 16.2 us: per_device(): lax.all_to_all(outgoing, ('tp', 'pool'), split_axis=0, concat_axis=0, til...]
    unnamed x19 -> x0, local copies, waits for them, and re-layouts: 10.9 us -> none
    all_to_all x2 -> x0, starting transfers between devices: 10.1 us -> none  [the longest x1 5.33 us: per_device(): lax.all_to_all(kv_weight, 'tp', split_axis=1, concat_axis=0, tiled=True)]
    slice x3 -> x0, local copies, waits for them, and re-layouts: 9.59 us -> none  [the longest x2 7.03 us: split_heads(): keys_part = stacked[:, :, :head_span].reshape(slot_count, -1, KVH, HD)]
    dot_general x7 -> x0, matrix products: 9.52 us -> none  [the longest x1 5.39 us: per_device(): product = jnp.dot(scaled, columns, preferred_element_type=jnp.float32)]
    all_to_all x2 -> x0, local copies, waits for them, and re-layouts: 8.39 us -> none  [the longest x1 7.87 us: per_device(): lax.all_to_all(kv_weight, 'tp', split_axis=1, concat_axis=0, tiled=True)]
  transfers between devices with their start and end apart: 3 -> 0, of which waited for: 1 -> 0; matrix products, arithmetic and copies ran while one was open for 15% -> 0% of each run, Pallas kernels for 0% -> 0%
where the time goes in v1:
time: 32.5 us; the launch traced here: 32.1 us
  Pallas kernels  28.1 us (86%)
  local copies, waits for them, and re-layouts  3.95 us (12%)
    pallas_call x1, Pallas kernels, per_device(): pl.pallas_call(functools.partial(kernel, n_tp, n_pool), out_shape=jax.Sha...  28.1 us
    reshape x1, local copies, waits for them, and re-layouts, per_device(): queries.reshape(slots * QH, HD)  1.34 us
    reshape x1, local copies, waits for them, and re-layouts, per_device(): return out.reshape(slots, QH * HD)  1.33 us
    reshape x1, local copies, waits for them, and re-layouts, per_device(): norm_gain.reshape(1, width)  1.28 us

profile of v1, /device:TPU:0, one launch (start us, length us, event | category | flops | bytes accessed | tf_op | source)
XLA Modules:
  0.0 32.1 jit_solution(6214713687378064784)
XLA Ops:
  0.0 1.3 %reshape.9.gain = bf16[1,1280]{1,0:T(2,128)(2,1)} reshape(bf16[1280]{0:T(1024)(128)(2,1)} %param.9) | data formatting | bytes 5120 | tf_op jit(solution)/shard_map/reshape | solution.py:321
  1.3 1.3 %reshape.10.q = bf16[64,128]{1,0:T(8,128)(2,1)} reshape(bf16[2,4096]{1,0:T(2,128)(2,1)} %param.12) | data formatting | bytes 32768 | tf_op jit(solution)/shard_map/reshape | solution.py:322
  2.6 28.1 %shard_map.82 = bf16[64,128]{1,0:T(8,128)(2,1)} custom-call(s32[32]{0:T(128)} %place.1, s32[32]{0:T(128)} %clen.1, s32[32]{0:T(128)} %fcnt.1, bf16[1,1280]{1,0:T(2,128)(2,1)} %reshape.9.gain, bf16[64,128]{1,0:T(8,128)(2,1)} %reshape.10.q, bf16[512,1280]{1,0:T(8,128)(2,1)} %frames_h.1, bf16[1280,2048]{1,0:T(8,128)(2,1)} %w_h.1, bf16[1024,2048]{1,0:T(8,128)(2,1)} %cache_h.1), custom_call_target="tpu_custom_call" | custom-call | tf_op jit(solution)/shard_map/pallas_call | solution.py:289
  30.7 1.3 %reshape.11 = bf16[2,4096]{1,0:T(2,128)(2,1)} reshape(bf16[64,128]{1,0:T(8,128)(2,1)} %shard_map.82) | data formatting | bytes 32768 | tf_op jit(solution)/shard_map/reshape | solution.py:323

commit v2 on v1

--- a/solution.py
+++ b/solution.py
@@ -47,10 +47,10 @@
 
 
 def kernel(n_tp, n_pool, place, clen, fcnt, gain, q, frames_h, w_h, cache_h, out,
-           fr, wk, wv, ca, xs, qt, qg, sendq, recvq, ssq, sg, lse, ob, sendo, recvo,
+           fr, wk, wv, ca, xs, qt, qg, sendq, recvq, ssq, sg, lse, sendo, recvo,
            sendp, recvp, oc,
            ld, s_tp, r_tp, s_pl, r_pl):
-    slots = q.shape[0] // QH
+    slots = q.shape[0]
     n_loc = fr.shape[0] // FRAMES
     per = n_loc // n_pool
     tiles = n_loc // PACK
@@ -100,7 +100,8 @@
             c.start()
         return made
 
-    qg[t] = q[...]
+    rows = [q[i:i + 1, h * HD:(h + 1) * HD].astype(F32) for i in range(slots) for h in range(QH)]
+    qg[t] = jnp.concatenate(rows, axis=0).astype(BF)
     pl.semaphore_wait(barrier, n_tp - 1 + n_pool - 1)
     hop = to_tp(0, lambda peer: qg.at[t], qg.at[t])
 
@@ -145,7 +146,7 @@
         mine.append(which)
 
     loads[0].wait()
-    gain_row = gain[...].astype(F32)
+    gain_row = gain[...].astype(F32).reshape(1, width)
     lane = iota((FRAMES, 128), 1)
 
     def scale_session(s, total):
@@ -166,7 +167,7 @@
 
     for s in range(n_loc // 2, n_loc):
         total = scale_session(s, total)
-    ssq[t] = total
+    ssq[t] = total.T[:n_loc]
     hop_sq = to_tp(1, lambda peer: ssq.at[t], ssq.at[t])
     loads[1].wait()
     for c in hop:
@@ -179,22 +180,21 @@
         for k in range(PACK):
             ids = jnp.where(lane // QH == k, order[a * PACK + k], ids)
         who.append(ids)
-        qt[:, a * 128:(a + 1) * 128] = lax.dot_general(
-            wk[...], spread_heads(group[a * 128:(a + 1) * 128]), NT,
-            preferred_element_type=F32).astype(BF)
+    qt[...] = lax.dot_general(wk[...], spread_heads(group), NT,
+                              preferred_element_type=F32).astype(BF)
     full = jnp.dot(xs[...], qt[...], preferred_element_type=F32)
     for a in range(tiles):
         packed = jnp.zeros((FRAMES, 128), F32)
         for s in range(n_loc):
             packed = jnp.where(who[a] == s, full[s * FRAMES:(s + 1) * FRAMES, a * 128:(a + 1) * 128],
                                packed)
-        sg[t, a * FRAMES:(a + 1) * FRAMES, :] = packed
+        sg[t, a * FRAMES:(a + 1) * FRAMES, :] = packed.astype(BF)
     hop = to_tp(2, lambda peer: sg.at[t], sg.at[t])
 
     loads[2].wait()
     tops, sums = [], []
     for i in range(slots):
-        qb = spread_heads(q[i * QH:(i + 1) * QH, :])
+        qb = spread_heads(qg[t, i * QH:(i + 1) * QH, :])
         rows = slice(i * SLOT_TOK, (i + 1) * SLOT_TOK)
         sc = lax.dot_general(qb, ca[rows, :HS], NT, preferred_element_type=F32) * scale
         sc = jnp.where(iota(sc.shape, 1) < lengths[i], sc, -1e30)
@@ -211,6 +211,7 @@
     for j in range(1, n_tp):
         squares = squares + ssq[j]
     inverse = lax.rsqrt(squares / (width * n_tp) + 1e-06)
+    inverse = jnp.concatenate([inverse, jnp.zeros((128 - n_loc, FRAMES), F32)], axis=0).T
     for c in hop:
         c.wait()
     weights = []
@@ -220,9 +221,9 @@
         for s in range(n_loc):
             inv = jnp.where(who[a] == s, inverse[:, s:s + 1], inv)
             valid = jnp.where(who[a] == s, fcnt[p * n_loc + s], valid)
-        sc = sg[0, a * FRAMES:(a + 1) * FRAMES, :]
+        sc = sg[0, a * FRAMES:(a + 1) * FRAMES, :].astype(F32)
         for j in range(1, n_tp):
-            sc = sc + sg[j, a * FRAMES:(a + 1) * FRAMES, :]
+            sc = sc + sg[j, a * FRAMES:(a + 1) * FRAMES, :].astype(F32)
         sc = jnp.where(iota(sc.shape, 0) < valid, sc * (inv * scale), -1e30)
         top = jnp.max(sc, axis=0, keepdims=True)
         pr = jnp.exp(sc - top)
@@ -234,13 +235,12 @@
     hop_l = to_pool(1, lambda peer: lse.at[p], lse.at[p])
 
     loads[3].wait()
-    for a in range(tiles):
-        wide = jnp.concatenate(
-            [jnp.where(who[a] == s, weights[a], 0.0) for s in range(n_loc)], axis=0)
-        y = jnp.dot(wide.T.astype(BF), xs[...], preferred_element_type=F32).astype(BF)
-        ob[a * 128:(a + 1) * 128, :] = gather_heads(
-            jnp.dot(y, wv[...], preferred_element_type=F32)).astype(BF)
-    sendo[...] = ob[...].reshape(n_pool, per * QH, HD)
+    wide = jnp.concatenate(
+        [jnp.concatenate([jnp.where(who[a] == s, weights[a], 0.0) for s in range(n_loc)], axis=0).T
+         for a in range(tiles)], axis=0)
+    y = jnp.dot(wide.astype(BF), xs[...], preferred_element_type=F32).astype(BF)
+    ob = gather_heads(jnp.dot(y, wv[...], preferred_element_type=F32)).astype(BF)
+    sendo[...] = ob.reshape(n_pool, per * QH, HD)
     recvo[p] = sendo[p]
     hop = to_pool(2, lambda peer: sendo.at[peer], recvo.at[p])
     for c in hop_l:
@@ -301,10 +301,9 @@
             pltpu.VMEM((n_tp, slots * QH, HD), BF),
             pltpu.VMEM((n_pool, per * QH, HD), BF),
             pltpu.VMEM((n_pool, per * QH, HD), BF),
-            pltpu.VMEM((n_tp, FRAMES, 128), F32),
-            pltpu.VMEM((n_tp, tiles * FRAMES, 128), F32),
+            pltpu.VMEM((n_tp, n_loc, FRAMES), F32),
+            pltpu.VMEM((n_tp, tiles * FRAMES, 128), BF),
             pltpu.VMEM((n_pool, max(8, tiles), 128), F32),
-            pltpu.VMEM((n_loc * QH, HD), BF),
             pltpu.VMEM((n_pool, per * QH, HD), BF),
             pltpu.VMEM((n_pool, per * QH, HD), BF),
             pltpu.VMEM((n_tp, slots * QH, HD), BF),
@@ -318,8 +317,8 @@
         ],
         compiler_params=pltpu.CompilerParams(
             collective_id=0, has_side_effects=True, vmem_limit_bytes=62 * 1024 * 1024),
-    )(placement, cached_len, frame_count, norm_gain.reshape(1, width),
-      queries.reshape(slots * QH, HD), frames, kv_weight, kv_cache)
+    )(placement, cached_len, frame_count, norm_gain,
+      queries, frames, kv_weight, kv_cache)
     return out.reshape(slots, QH * HD)
 
 

time: 32.5 us -> 29.1 us (0.90)
  local copies, waits for them, and re-layouts: 3.95 us -> 1.33 us
  Pallas kernels: 28.1 us -> 27.5 us
    reshape x2 -> x0, local copies, waits for them, and re-layouts: 2.62 us -> none  [the longest x1 1.34 us: per_device(): queries.reshape(slots * QH, HD)]
    pallas_call x1, Pallas kernels: 28.1 us -> 27.5 us  [per_device(): pl.pallas_call(functools.partial(kernel, n_tp, n_pool), out_shape=jax.Sha...]
where the time goes in v2:
time: 29.1 us; the launch traced here: 28.8 us
  Pallas kernels  27.5 us (95%)
  local copies, waits for them, and re-layouts  1.33 us (5%)
    pallas_call x1, Pallas kernels, per_device(): pl.pallas_call(functools.partial(kernel, n_tp, n_pool), out_shape=jax.Sha...  27.5 us
    reshape x1, local copies, waits for them, and re-layouts, per_device(): return out.reshape(slots, QH * HD)  1.33 us

profile of v2, /device:TPU:0, one launch (start us, length us, event | category | flops | bytes accessed | tf_op | source)
XLA Modules:
  0.0 28.8 jit_solution(6611325310879950580)
XLA Ops:
  0.0 27.5 %shard_map.82 = bf16[64,128]{1,0:T(8,128)(2,1)} custom-call(s32[32]{0:T(128)} %place.1, s32[32]{0:T(128)} %clen.1, s32[32]{0:T(128)} %fcnt.1, bf16[1280]{0:T(1024)(128)(2,1)} %gain.1, bf16[2,4096]{1,0:T(2,128)(2,1)} %q.1, bf16[512,1280]{1,0:T(8,128)(2,1)} %frames_h.1, bf16[1280,2048]{1,0:T(8,128)(2,1)} %w_h.1, bf16[1024,2048]{1,0:T(8,128)(2,1)} %cache_h.1), custom_call_target="tpu_custom_call" | custom-call | tf_op jit(solution)/shard_map/pallas_call | solution.py:289
  27.5 1.3 %reshape.3 = bf16[2,4096]{1,0:T(2,128)(2,1)} reshape(bf16[64,128]{1,0:T(8,128)(2,1)} %shard_map.82) | data formatting | bytes 32768 | tf_op jit(solution)/shard_map/reshape | solution.py:322

commit v3 on v2

--- a/solution.py
+++ b/solution.py
@@ -47,7 +47,7 @@
 
 
 def kernel(n_tp, n_pool, place, clen, fcnt, gain, q, frames_h, w_h, cache_h, out,
-           fr, wk, wv, ca, xs, qt, qg, sendq, recvq, ssq, sg, lse, sendo, recvo,
+           fr, wk, wv, ca, xs, kp, vp, qg, sendq, recvq, ssq, sg, lse, sendo, recvo,
            sendp, recvp, oc,
            ld, s_tp, r_tp, s_pl, r_pl):
     slots = q.shape[0]
@@ -118,6 +118,28 @@
                 found[k] = jnp.where(match & (count == k), key, found[k])
             count = count + match.astype(jnp.int32)
         keys += found
+    loads[0].wait()
+    gain_row = gain[...].astype(F32).reshape(1, width)
+    lane = iota((FRAMES, 128), 1)
+
+    def scale_session(s, total):
+        x = fr[s * FRAMES:(s + 1) * FRAMES, :].astype(F32)
+        xs[s * FRAMES:(s + 1) * FRAMES, :] = (x * gain_row).astype(BF)
+        return jnp.where(lane == s, jnp.sum(x * x, axis=1, keepdims=True), total)
+
+    total = jnp.zeros((FRAMES, 128), F32)
+    for s in range(n_loc):
+        total = scale_session(s, total)
+
+    ssq[t] = total.T[:n_loc]
+    hop_sq = to_tp(1, lambda peer: ssq.at[t], ssq.at[t])
+    for c in hop:
+        c.wait()
+    moved = permute(keys, qg[...].reshape(n_tp * slots * QH, HD))
+    sendq[...] = moved.reshape(n_pool, per * QH, HD)
+    recvq[p] = sendq[p]
+    hop = to_pool(0, lambda peer: sendq.at[peer], recvq.at[p])
+
     held = []
     for o in range(n_tp * slots):
         which = jnp.int32(-1)
@@ -145,31 +167,10 @@
         lengths.append(length)
         mine.append(which)
 
-    loads[0].wait()
-    gain_row = gain[...].astype(F32).reshape(1, width)
-    lane = iota((FRAMES, 128), 1)
-
-    def scale_session(s, total):
-        x = fr[s * FRAMES:(s + 1) * FRAMES, :].astype(F32)
-        xs[s * FRAMES:(s + 1) * FRAMES, :] = (x * gain_row).astype(BF)
-        return jnp.where(lane == s, jnp.sum(x * x, axis=1, keepdims=True), total)
-
-    total = jnp.zeros((FRAMES, 128), F32)
-    for s in range(n_loc // 2):
-        total = scale_session(s, total)
-
-    for c in hop:
-        c.wait()
-    moved = permute(keys, qg[...].reshape(n_tp * slots * QH, HD))
-    sendq[...] = moved.reshape(n_pool, per * QH, HD)
-    recvq[p] = sendq[p]
-    hop = to_pool(0, lambda peer: sendq.at[peer], recvq.at[p])
-
-    for s in range(n_loc // 2, n_loc):
-        total = scale_session(s, total)
-    ssq[t] = total.T[:n_loc]
-    hop_sq = to_tp(1, lambda peer: ssq.at[t], ssq.at[t])
     loads[1].wait()
+    for s in range(0, n_loc, PACK):
+        rows = slice(s * FRAMES, (s + PACK) * FRAMES)
+        kp[rows, :] = jnp.dot(xs[rows, :], wk[...], preferred_element_type=F32).astype(BF)
     for c in hop:
         c.wait()
 
@@ -180,9 +181,7 @@
         for k in range(PACK):
             ids = jnp.where(lane // QH == k, order[a * PACK + k], ids)
         who.append(ids)
-    qt[...] = lax.dot_general(wk[...], spread_heads(group), NT,
-                              preferred_element_type=F32).astype(BF)
-    full = jnp.dot(xs[...], qt[...], preferred_element_type=F32)
+    full = lax.dot_general(kp[...], spread_heads(group), NT, preferred_element_type=F32)
     for a in range(tiles):
         packed = jnp.zeros((FRAMES, 128), F32)
         for s in range(n_loc):
@@ -191,19 +190,10 @@
         sg[t, a * FRAMES:(a + 1) * FRAMES, :] = packed.astype(BF)
     hop = to_tp(2, lambda peer: sg.at[t], sg.at[t])
 
-    loads[2].wait()
-    tops, sums = [], []
-    for i in range(slots):
-        qb = spread_heads(qg[t, i * QH:(i + 1) * QH, :])
-        rows = slice(i * SLOT_TOK, (i + 1) * SLOT_TOK)
-        sc = lax.dot_general(qb, ca[rows, :HS], NT, preferred_element_type=F32) * scale
-        sc = jnp.where(iota(sc.shape, 1) < lengths[i], sc, -1e30)
-        top = jnp.max(sc, axis=1, keepdims=True)
-        pr = jnp.exp(sc - top)
-        tops.append(top)
-        sums.append(jnp.sum(pr, axis=1, keepdims=True))
-        oc[i * QH:(i + 1) * QH, :] = gather_heads(
-            jnp.dot(pr.astype(BF), ca[rows, HS:], preferred_element_type=F32))
+    loads[3].wait()
+    for s in range(0, n_loc, PACK):
+        rows = slice(s * FRAMES, (s + PACK) * FRAMES)
+        vp[rows, :] = jnp.dot(xs[rows, :], wv[...], preferred_element_type=F32).astype(BF)
 
     for c in hop_sq:
         c.wait()
@@ -234,15 +224,31 @@
         lse[p, tiles:, :] = jnp.zeros((lse.shape[1] - tiles, 128), F32)
     hop_l = to_pool(1, lambda peer: lse.at[p], lse.at[p])
 
-    loads[3].wait()
     wide = jnp.concatenate(
         [jnp.concatenate([jnp.where(who[a] == s, weights[a], 0.0) for s in range(n_loc)], axis=0).T
          for a in range(tiles)], axis=0)
-    y = jnp.dot(wide.astype(BF), xs[...], preferred_element_type=F32).astype(BF)
-    ob = gather_heads(jnp.dot(y, wv[...], preferred_element_type=F32)).astype(BF)
+    ob = gather_heads(jnp.dot(wide.astype(BF), vp[...], preferred_element_type=F32)).astype(BF)
     sendo[...] = ob.reshape(n_pool, per * QH, HD)
     recvo[p] = sendo[p]
     hop = to_pool(2, lambda peer: sendo.at[peer], recvo.at[p])
+
+    loads[2].wait()
+    tops, sums = [], []
+
+    def attend_cached(i):
+        qb = spread_heads(qg[t, i * QH:(i + 1) * QH, :])
+        rows = slice(i * SLOT_TOK, (i + 1) * SLOT_TOK)
+        sc = lax.dot_general(qb, ca[rows, :HS], NT, preferred_element_type=F32) * scale
+        sc = jnp.where(iota(sc.shape, 1) < lengths[i], sc, -1e30)
+        top = jnp.max(sc, axis=1, keepdims=True)
+        pr = jnp.exp(sc - top)
+        tops.append(top)
+        sums.append(jnp.sum(pr, axis=1, keepdims=True))
+        oc[i * QH:(i + 1) * QH, :] = gather_heads(
+            jnp.dot(pr.astype(BF), ca[rows, HS:], preferred_element_type=F32))
+
+    for i in range(slots // 2):
+        attend_cached(i)
     for c in hop_l:
         c.wait()
     fresh_lse = []
@@ -262,6 +268,8 @@
     sendp[...] = moved.reshape(n_tp, slots * QH, HD)
     recvp[t] = sendp[t]
     hop = to_tp(3, lambda peer: sendp.at[peer], recvp.at[t])
+    for i in range(slots // 2, slots):
+        attend_cached(i)
     for c in hop:
         c.wait()
     for i in range(slots):
@@ -297,7 +305,8 @@
             pltpu.VMEM((width, HS), BF),
             pltpu.VMEM(kv_cache.shape, BF),
             pltpu.VMEM((rows, width), BF),
-            pltpu.VMEM((width, n_loc * QH), BF),
+            pltpu.VMEM((rows, HS), BF),
+            pltpu.VMEM((rows, HS), BF),
             pltpu.VMEM((n_tp, slots * QH, HD), BF),
             pltpu.VMEM((n_pool, per * QH, HD), BF),
             pltpu.VMEM((n_pool, per * QH, HD), BF),

time: 29.1 us -> 27.2 us (0.935)
  Pallas kernels: 27.5 us -> 25.5 us
    pallas_call x1, Pallas kernels: 27.5 us -> 25.5 us  [per_device(): pl.pallas_call(functools.partial(kernel, n_tp, n_pool), out_shape=jax.Sha...]
where the time goes in v3:
time: 27.2 us; the launch traced here: 26.9 us
  Pallas kernels  25.5 us (94%)
  local copies, waits for them, and re-layouts  1.33 us (5%)
    pallas_call x1, Pallas kernels, per_device(): pl.pallas_call(functools.partial(kernel, n_tp, n_pool), out_shape=jax.Sha...  25.5 us
    reshape x1, local copies, waits for them, and re-layouts, per_device(): return out.reshape(slots, QH * HD)  1.33 us

profile of v3, /device:TPU:0, one launch (start us, length us, event | category | flops | bytes accessed | tf_op | source)
XLA Modules:
  0.0 26.9 jit_solution(15737490560574686966)
XLA Ops:
  0.0 25.5 %shard_map.82 = bf16[64,128]{1,0:T(8,128)(2,1)} custom-call(s32[32]{0:T(128)} %place.1, s32[32]{0:T(128)} %clen.1, s32[32]{0:T(128)} %fcnt.1, bf16[1280]{0:T(1024)(128)(2,1)} %gain.1, bf16[2,4096]{1,0:T(2,128)(2,1)} %q.1, bf16[512,1280]{1,0:T(8,128)(2,1)} %frames_h.1, bf16[1280,2048]{1,0:T(8,128)(2,1)} %w_h.1, bf16[1024,2048]{1,0:T(8,128)(2,1)} %cache_h.1), custom_call_target="tpu_custom_call" | custom-call | tf_op jit(solution)/shard_map/pallas_call | solution.py:297
  25.5 1.3 %reshape.3 = bf16[2,4096]{1,0:T(2,128)(2,1)} reshape(bf16[64,128]{1,0:T(8,128)(2,1)} %shard_map.82) | data formatting | bytes 32768 | tf_op jit(solution)/shard_map/reshape | solution.py:331

commit v4 on v3

--- a/solution.py
+++ b/solution.py
@@ -168,8 +168,8 @@
         mine.append(which)
 
     loads[1].wait()
-    for s in range(0, n_loc, PACK):
-        rows = slice(s * FRAMES, (s + PACK) * FRAMES)
+    for s in range(0, n_loc, 2 * PACK):
+        rows = slice(s * FRAMES, (s + 2 * PACK) * FRAMES)
         kp[rows, :] = jnp.dot(xs[rows, :], wk[...], preferred_element_type=F32).astype(BF)
     for c in hop:
         c.wait()
@@ -191,8 +191,8 @@
     hop = to_tp(2, lambda peer: sg.at[t], sg.at[t])
 
     loads[3].wait()
-    for s in range(0, n_loc, PACK):
-        rows = slice(s * FRAMES, (s + PACK) * FRAMES)
+    for s in range(0, n_loc, 2 * PACK):
+        rows = slice(s * FRAMES, (s + 2 * PACK) * FRAMES)
         vp[rows, :] = jnp.dot(xs[rows, :], wv[...], preferred_element_type=F32).astype(BF)
 
     for c in hop_sq:

time: 27.2 us -> 27.3 us (level)
  no operation moved by 1% of the time
where the time goes in v4:
time: 27.3 us; the launch traced here: 27 us
  Pallas kernels  25.6 us (94%)
  local copies, waits for them, and re-layouts  1.33 us (5%)
    pallas_call x1, Pallas kernels, per_device(): pl.pallas_call(functools.partial(kernel, n_tp, n_pool), out_shape=jax.Sha...  25.6 us
    reshape x1, local copies, waits for them, and re-layouts, per_device(): return out.reshape(slots, QH * HD)  1.33 us

profile of v4, /device:TPU:0, one launch (start us, length us, event | category | flops | bytes accessed | tf_op | source)
XLA Modules:
  0.0 27.0 jit_solution(17438178828879212737)
XLA Ops:
  0.0 25.6 %shard_map.82 = bf16[64,128]{1,0:T(8,128)(2,1)} custom-call(s32[32]{0:T(128)} %place.1, s32[32]{0:T(128)} %clen.1, s32[32]{0:T(128)} %fcnt.1, bf16[1280]{0:T(1024)(128)(2,1)} %gain.1, bf16[2,4096]{1,0:T(2,128)(2,1)} %q.1, bf16[512,1280]{1,0:T(8,128)(2,1)} %frames_h.1, bf16[1280,2048]{1,0:T(8,128)(2,1)} %w_h.1, bf16[1024,2048]{1,0:T(8,128)(2,1)} %cache_h.1), custom_call_target="tpu_custom_call" | custom-call | tf_op jit(solution)/shard_map/pallas_call | solution.py:297
  25.7 1.3 %reshape.3 = bf16[2,4096]{1,0:T(2,128)(2,1)} reshape(bf16[64,128]{1,0:T(8,128)(2,1)} %shard_map.82) | data formatting | bytes 32768 | tf_op jit(solution)/shard_map/reshape | solution.py:331
